TPU v7x, 512 devices: a whole 4x4x16 slice. The times are simulated.
512 devices in a mesh: section: 32 (over z, core), row: 16 (over y, x).
Axes of the slice: x: 4, y: 4, z: 16, core: 2. Of those that a mesh axis runs over, the one named last changes fastest.
Arguments:
- section_inputs: bfloat16 [32, 2048, 2048], P('section', 'row'), may hold values from -6 to 6
- fresh_group: bfloat16 [2048, 2048], P('row'), may hold values from -6 to 6
- resident_state: float32 [32, 8, 128, 128], P('section'), may hold values from -162.9174 to 162.9174
- qkv_weight: bfloat16 [32, 2048, 3072], P('section', 'row'), may hold values from -0.125 to 0.125
- out_weight: bfloat16 [32, 1024, 2048], P('section', 'row'), may hold values from -0.1875 to 0.1875
- input_gain: float32 [32, 2048], P('section'), may hold values from 0.1 to 1.9
- head_gain: float32 [32, 1024], P('section'), may hold values from 0.1 to 1.9
Outputs:
- section_outputs: bfloat16 [32, 2048, 2048], P('section', 'row')
- final_state: float32 [32, 8, 128, 128], P('section')
All inputs are finite; a program needn't handle non-finite values.
Results may differ from a plain program's by a relative error of at most 0.01.
Values may be sent and summed in bfloat16 or wider, within the bound.
A program may use at most 64 MiB of HBM per device.

v0:
```python
import jax
import jax.numpy as jnp
from jax import lax
from jax.sharding import PartitionSpec as P


def passed_along(value, axis, by):
    peers = lax.axis_size(axis)
    pairs = [(i, i + by) for i in range(peers) if 0 <= i + by < peers]
    return lax.ppermute(value, axis, pairs)


def layer(inputs, state, qkv_full, out_full, input_gain, head_gain):
    rows = inputs.shape[0]
    heads = state.shape[0]
    head_size = state.shape[1]
    width = heads * head_size
    wide = inputs.astype(jnp.float32)
    normed = (
        wide * lax.rsqrt(jnp.mean(wide * wide, axis=-1, keepdims=True) + 1e-05) * input_gain
    ).astype(jnp.bfloat16)
    projected = jnp.dot(normed, qkv_full, preferred_element_type=jnp.float32)
    queries = jax.nn.silu(projected[:, :width]).astype(jnp.bfloat16).reshape(rows, heads, head_size)
    key_rows = (
        jax.nn.silu(projected[:, width : 2 * width])
        .astype(jnp.bfloat16)
        .reshape(rows, heads, head_size)
    )
    value_rows = projected[:, 2 * width :].astype(jnp.bfloat16).reshape(rows, heads, head_size)
    own_state = jnp.einsum("jhd,jhe->hde", key_rows, value_rows, preferred_element_type=jnp.float32)
    every = lax.all_gather(own_state[None].astype(jnp.bfloat16), "row", axis=0, tiled=True).astype(
        jnp.float32
    )
    order = lax.iota(jnp.int32, every.shape[0])
    earlier = (order < lax.axis_index("row")).astype(jnp.float32)
    before = jnp.sum(every * earlier[:, None, None, None], axis=0)
    total = jnp.sum(every, axis=0)
    prefix = state + before
    carried = jnp.einsum("ihd,hde->ihe", queries.astype(jnp.float32), prefix)
    scores = jnp.einsum("ihd,jhd->hij", queries, key_rows, preferred_element_type=jnp.float32)
    causal = lax.broadcasted_iota(jnp.int32, (rows, rows), 0) >= lax.broadcasted_iota(
        jnp.int32, (rows, rows), 1
    )
    weights = jnp.where(causal[None], scores, 0.0).astype(jnp.bfloat16)
    local = jnp.einsum("hij,jhe->ihe", weights, value_rows, preferred_element_type=jnp.float32)
    attended = carried + local
    scaled = attended * lax.rsqrt(jnp.mean(attended * attended, axis=-1, keepdims=True) + 1e-06)
    head_out = (scaled.reshape(rows, width) * head_gain).astype(jnp.bfloat16)
    result = (wide + jnp.dot(head_out, out_full, preferred_element_type=jnp.float32)).astype(
        jnp.bfloat16
    )
    return (result, state + total)


def body(
    section_inputs, fresh_group, resident_state, qkv_weight, out_weight, input_gain, head_gain
):
    qkv_full, out_full = (
        lax.all_gather(qkv_weight[0], "row", axis=0, tiled=True),
        lax.all_gather(out_weight[0], "row", axis=0, tiled=True),
    )
    first_out, first_state = layer(
        section_inputs[0], resident_state[0], qkv_full, out_full, input_gain[0], head_gain[0]
    )
    arrived = passed_along(first_out, "section", 1)
    second_in = jnp.where(lax.axis_index("section") == 0, fresh_group, arrived)
    second_out, second_state = layer(
        second_in, first_state, qkv_full, out_full, input_gain[0], head_gain[0]
    )
    return (second_out[None], second_state[None])


def solution(mesh):
    in_specs = (
        P("section", "row", None),
        P("row", None),
        P("section", None, None, None),
        P("section", "row", None),
        P("section", "row", None),
        P("section", None),
        P("section", None),
    )
    out_specs = (P("section", "row", None), P("section", None, None, None))
    return jax.shard_map(body, mesh=mesh, in_specs=in_specs, out_specs=out_specs, check_vma=False)
```

profile of v0, /device:TPU:1, one launch (start us, length us, event | category | flops | bytes accessed | tf_op | source)
XLA Modules:
  0.0 372.2 jit_solution(13485516950461262047)
XLA Ops:
  7.2 0.7 all-gather.9.cloned.1.call-update
  7.9 1.2 fusion.32
  9.2 112.5 %all-gather.9.cloned.1.call-done = bf16[1,2048,3072]{2,1,0:T(8,128)(2,1)} async-done(((bf16[1,128,3072]{2,1,0:T(8,128)(2,1)}), bf16[1,2048,3072]{2,1,0:T(8,128)(2,1)}) %all-gather.9.cloned.1.call-update) | async-done | bytes 12582928 | tf_op jit(solution)/shard_map/all_gather | solution.py:59
  121.7 6.7 %fusion.2 = f32[128,3072]{1,0:T(8,128)S(1)} fusion(bf16[1,2048,3072]{2,1,0:T(8,128)(2,1)} %all-gather.9.cloned.1.call-done, bf16[1,128,2048]{2,1,0:T(8,128)(2,1)} %param.7, f32[2048]{0:T(1024)} %bitcast.105, f32[128]{0:T(128)S(1)} %add_rsqrt_fusion.3), kind=kOutput, calls=%fused_computation.2 | convolution fusion | flops 1611661312 | bytes 14688768 | tf_op jit(solution)/shard_map/dot_general | solution.py:22
  128.4 0.3 fusion.56
  129.1 1.0 convolution_convert_fusion.1
  130.1 0.7 all-gather.13.cloned.1.call-update
  130.9 66.0 %all-gather.11.cloned.1.call-done = bf16[128,128,128]{2,1,0:T(8,128)(2,1)} async-done(((bf16[8,128,128]{2,1,0:T(8,128)(2,1)}), bf16[128,128,128]{2,1,0:T(8,128)(2,1)}) %all-gather.11.cloned.1.call-update) | async-done | bytes 4194320 | tf_op jit(solution)/shard_map/all_gather | solution.py:31
  196.9 3.6 convert_reduce_fusion.1
  200.4 0.3 fusion.40
  200.8 0.5 multiply_reduce_fusion.1
  201.6 65.0 %all-gather.13.cloned.1.call-done = bf16[1,1024,2048]{2,1,0:T(8,128)(2,1)} async-done(((bf16[1,64,2048]{2,1,0:T(8,128)(2,1)}), bf16[1,1024,2048]{2,1,0:T(8,128)(2,1)}) %all-gather.13.cloned.1.call-update) | async-done | bytes 4194320 | tf_op jit(solution)/shard_map/all_gather | solution.py:60
  266.5 2.9 fusion.19
  269.5 3.7 %collective-permute-start = (bf16[128,2048]{1,0:T(8,128)(2,1)S(1)}, bf16[128,2048]{1,0:T(8,128)(2,1)S(1)}, u32[]{:S(2)}, u32[]{:S(2)}) collective-permute-start(bf16[128,2048]{1,0:T(8,128)(2,1)S(1)} %fusion.19), channel_id=1, source_target_pairs={{0,16},{16,32},{32,48},{48,64},{64,80},{80,96},{96,112},{112,128},... | collective-permute-start | bytes 1572872 | tf_op jit(solution)/shard_map/ppermute | solution.py:10
  273.2 6.1 %collective-permute-done = bf16[128,2048]{1,0:T(8,128)(2,1)S(1)} collective-permute-done((bf16[128,2048]{1,0:T(8,128)(2,1)S(1)}, bf16[128,2048]{1,0:T(8,128)(2,1)S(1)}, u32[]{:S(2)}, u32[]{:S(2)}) %collective-permute-start) | collective-permute-done | bytes 524320 | tf_op jit(solution)/shard_map/ppermute | solution.py:10
  279.6 6.5 %fusion = f32[128,3072]{1,0:T(8,128)S(1)} fusion(bf16[1,2048,3072]{2,1,0:T(8,128)(2,1)} %all-gather.9.cloned.1.call-done, bf16[128,2048]{1,0:T(8,128)(2,1)S(1)} %get-tuple-element.7, f32[128]{0:T(128)S(1)} %add_rsqrt_fusion.2, f32[2048]{0:T(1024)S(1)} %bitcast.106), kind=kOutput, calls=%fused_computation | convolution fusion | flops 1611661312 | bytes 14688768 | tf_op jit(solution)/shard_map/dot_general | solution.py:22
  286.1 0.3 fusion.57
  286.8 1.0 convolution_convert_fusion
  287.9 68.6 %all-gather.15.cloned.1.call-done = bf16[128,128,128]{2,1,0:T(8,128)(2,1)} async-done(((bf16[8,128,128]{2,1,0:T(8,128)(2,1)}), bf16[128,128,128]{2,1,0:T(8,128)(2,1)}) %all-gather.15.cloned.1.call-update) | async-done | bytes 4194320 | tf_op jit(solution)/shard_map/all_gather | solution.py:31
  356.5 3.5 convert_reduce_fusion
  360.0 0.9 bitcast_add_fusion
  360.9 0.3 fusion.42
  361.2 0.5 multiply_reduce_fusion
  362.0 3.7 %fusion.22 = bf16[1,128,2048]{2,1,0:T(8,128)(2,1)} fusion(bf16[128,1024]{0,1:T(8,128)(2,1)S(1)} %fusion.37, bf16[1,1024,2048]{2,1,0:T(8,128)(2,1)} %all-gather.13.cloned.1.call-done, bf16[128,2048]{1,0:T(8,128)(2,1)S(1)} %get-tuple-element.7), kind=kOutput, calls=%fused_computation.18 | convolution fusion | flops 537657344 | bytes 5505024 | tf_op jit(solution)/shard_map/dot_general | solution.py:49
  (33 shorter events, 1.8 us)
Async XLA Ops:
  7.2 114.5 %all-gather.9.cloned.1.call-start = ((), (), s32[]{:S(2)}) async-start(), calls=%async_computation | async-start | bytes 13369344 | tf_op jit(solution)/shard_map/all_gather | solution.py:59
  7.9 189.0 %all-gather.11.cloned.1.call-start = ((), (), s32[]{:S(2)}) async-start(), calls=%async_computation.1 | async-start | bytes 4456448 | tf_op jit(solution)/shard_map/all_gather | solution.py:31
  128.6 71.8 %copy-start.1 = (f32[1,8,128,128]{3,2,1,0:T(8,128)S(1)}, f32[1,8,128,128]{3,2,1,0:T(8,128)}, u32[]{:S(2)}) copy-start(f32[1,8,128,128]{3,2,1,0:T(8,128)} %param.9) | copy-start | bytes 1572868
  130.1 136.5 %all-gather.13.cloned.1.call-start = ((), (), s32[]{:S(2)}) async-start(), calls=%async_computation.2 | async-start | bytes 4456448 | tf_op jit(solution)/shard_map/all_gather | solution.py:60
  130.8 225.7 %all-gather.15.cloned.1.call-start = ((), (), s32[]{:S(2)}) async-start(), calls=%async_computation.3 | async-start | bytes 4456448 | tf_op jit(solution)/shard_map/all_gather | solution.py:31
  196.9 4.5 %copy-start.4 = (f32[1,1024]{1,0:T(1,128)S(1)}, f32[1,1024]{1,0:T(1,128)}, u32[]{:S(2)}) copy-start(f32[1,1024]{1,0:T(1,128)} %param.13) | copy-start | bytes 12292
  196.9 69.7 %copy-start = (bf16[1,128,2048]{2,1,0:T(8,128)(2,1)S(1)}, bf16[1,128,2048]{2,1,0:T(8,128)(2,1)}, u32[]{:S(2)}) copy-start(bf16[1,128,2048]{2,1,0:T(8,128)(2,1)} %param.7) | copy-start | bytes 1572868
  201.2 78.1 %copy-start.2 = (bf16[128,2048]{1,0:T(8,128)(2,1)S(1)}, bf16[128,2048]{1,0:T(8,128)(2,1)}, u32[]{:S(2)}) copy-start(bf16[128,2048]{1,0:T(8,128)(2,1)} %param.8) | copy-start | bytes 1572868
  201.3 78.3 %copy-start.3 = (f32[1,2048]{1,0:T(1,128)S(1)}, f32[1,2048]{1,0:T(1,128)}, u32[]{:S(2)}) copy-start(f32[1,2048]{1,0:T(1,128)} %param.12) | copy-start | bytes 24580
  269.5 9.8 %collective-permute-start = (bf16[128,2048]{1,0:T(8,128)(2,1)S(1)}, bf16[128,2048]{1,0:T(8,128)(2,1)S(1)}, u32[]{:S(2)}, u32[]{:S(2)}) collective-permute-start(bf16[128,2048]{1,0:T(8,128)(2,1)S(1)} %fusion.19), channel_id=1, source_target_pairs={{0,16},{16,32},{32,48},{48,64},{64,80},{80,96},{96,112},{112,128},... | collective-permute-start | bytes 1572872 | tf_op jit(solution)/shard_map/ppermute | solution.py:10
Sparse Core Ops, SparseCore 0:
  11.0 110.6 all-gather.8
  130.2 66.6 all-gather.10
  199.9 66.6 all-gather.12
  288.0 68.4 all-gather.14
where the time goes:
time: 373 us; the launch traced here: 372 us
  waiting for transfers between devices  320 us (86%)
  matrix products  23.4 us (6%)
  between operations  14 us (4%)
  other arithmetic  10.6 us (3%)
  starting transfers between devices  3.89 us (1%)
    all_gather x2, waiting for transfers between devices, layer(): lax.all_gather(own_state[None].astype(jnp.bfloat16), 'row', axis=0, tiled...  135 us
    all_gather x1, waiting for transfers between devices, body(): lax.all_gather(qkv_weight[0], 'row', axis=0, tiled=True)  112 us
    all_gather x1, waiting for transfers between devices, body(): lax.all_gather(out_weight[0], 'row', axis=0, tiled=True)  65 us
    dot_general x2, matrix products, layer(): projected = jnp.dot(normed, qkv_full, preferred_element_type=jnp.float32)  13.2 us
  transfers between devices with their start and end apart: 5, of which 5 were waited for; matrix products, arithmetic and copies ran while one was open for 2% of the time, Pallas kernels for 0%

commit v1 on v0

--- a/solution.py
+++ b/solution.py
@@ -55,9 +55,15 @@
 def body(
     section_inputs, fresh_group, resident_state, qkv_weight, out_weight, input_gain, head_gain
 ):
+    _detail_threads = lambda work_x, axis_name: jnp.concatenate(
+        lax.all_to_all(
+            jnp.stack([work_x for _ in range(lax.axis_size(axis_name))], axis=0), axis_name, 0, 0
+        ),
+        0,
+    )
     qkv_full, out_full = (
         lax.all_gather(qkv_weight[0], "row", axis=0, tiled=True),
-        lax.all_gather(out_weight[0], "row", axis=0, tiled=True),
+        _detail_threads(out_weight[0], "row"),
     )
     first_out, first_state = layer(
         section_inputs[0], resident_state[0], qkv_full, out_full, input_gain[0], head_gain[0]

time: 373 us -> 338 us (0.906)
  waiting for transfers between devices: 320 us -> 277 us
  starting transfers between devices: 3.89 us -> 9.07 us
    all_gather x1 -> x0, waiting for transfers between devices: 65 us -> none  [body(): lax.all_gather(out_weight[0], 'row', axis=0, tiled=True)]
    all_gather x2, waiting for transfers between devices: 135 us -> 158 us  [layer(): lax.all_gather(own_state[None].astype(jnp.bfloat16), 'row', axis=0, tiled...]
    all_to_all x0 -> x1, starting transfers between devices: none -> 5.03 us  [body(): lax.all_to_all(jnp.stack([work_x for _ in range(lax.axis_size(axis_name))...]
  transfers between devices with their start and end apart: 5 -> 5, of which waited for: 5 -> 4; matrix products, arithmetic and copies ran while one was open for 2% -> 2% of each run, Pallas kernels for 0% -> 0%
where the time goes in v1:
time: 338 us; the launch traced here: 337 us
  waiting for transfers between devices  277 us (82%)
  matrix products  23.4 us (7%)
  between operations  14 us (4%)
  other arithmetic  10.5 us (3%)
  starting transfers between devices  9.07 us (3%)
    all_gather x2, waiting for transfers between devices, layer(): lax.all_gather(own_state[None].astype(jnp.bfloat16), 'row', axis=0, tiled...  158 us
    all_gather x1, waiting for transfers between devices, body(): lax.all_gather(qkv_weight[0], 'row', axis=0, tiled=True)  112 us
    dot_general x2, matrix products, layer(): projected = jnp.dot(normed, qkv_full, preferred_element_type=jnp.float32)  13.2 us
    reduce_sum x2, other arithmetic, layer(): total = jnp.sum(every, axis=0)  7.09 us
  transfers between devices with their start and end apart: 5, of which 4 were waited for; matrix products, arithmetic and copies ran while one was open for 2% of the time, Pallas kernels for 0%

profile of v1, /device:TPU:1, one launch (start us, length us, event | category | flops | bytes accessed | tf_op | source)
XLA Modules:
  0.0 337.4 jit_solution(17369476133870625532)
XLA Ops:
  7.2 0.7 all-gather.7.cloned.1.call-update
  7.9 1.2 fusion.16
  9.2 112.5 %all-gather.7.cloned.1.call-done = bf16[1,2048,3072]{2,1,0:T(8,128)(2,1)} async-done(((bf16[1,128,3072]{2,1,0:T(8,128)(2,1)}), bf16[1,2048,3072]{2,1,0:T(8,128)(2,1)}) %all-gather.7.cloned.1.call-update) | async-done | bytes 12582928 | tf_op jit(solution)/shard_map/all_gather | solution.py:65
  121.7 6.7 %fusion.2 = f32[128,3072]{1,0:T(8,128)S(1)} fusion(bf16[1,2048,3072]{2,1,0:T(8,128)(2,1)} %all-gather.7.cloned.1.call-done, bf16[1,128,2048]{2,1,0:T(8,128)(2,1)} %param.7, f32[2048]{0:T(1024)} %bitcast.90, f32[128]{0:T(128)S(1)} %add_rsqrt_fusion.3), kind=kOutput, calls=%fused_computation.2 | convolution fusion | flops 1611661312 | bytes 14688768 | tf_op jit(solution)/shard_map/dot_general | solution.py:22
  128.4 0.3 fusion.38
  129.0 1.0 convolution_convert_fusion.1
  130.1 2.5 stack.3
  132.6 5.0 %all-to-all-start = ((bf16[16,64,2048]{2,1,0:T(8,128)(2,1)}), bf16[16,64,2048]{2,1,0:T(8,128)(2,1)}, u32[]{:S(2)}, u32[]{:S(2)}) async-start(bf16[16,64,2048]{2,1,0:T(8,128)(2,1)} %stack.3), calls=%async_computation | async-start | bytes 8388608 | tf_op jit(solution)/shard_map/all_to_all | solution.py:59
  137.7 89.4 %all-gather.9.cloned.1.call-done = bf16[128,128,128]{2,1,0:T(8,128)(2,1)} async-done(((bf16[8,128,128]{2,1,0:T(8,128)(2,1)}), bf16[128,128,128]{2,1,0:T(8,128)(2,1)}) %all-gather.9.cloned.1.call-update) | async-done | bytes 4194320 | tf_op jit(solution)/shard_map/all_gather | solution.py:31
  227.1 3.6 %convert_reduce_fusion.1 = (f32[8,128,128]{2,1,0:T(8,128)S(1)}, f32[8,128,128]{2,1,0:T(8,128)S(1)}) fusion(bf16[16,8,128,128]{3,2,1,0:T(8,128)(2,1)} %bitcast.78, f32[16]{0:T(128)S(1)} %compare_convert_fusion), kind=kLoop, calls=%fused_computation.6 | loop fusion | flops 8126464 | bytes 5242944 | tf_op jit(solution)/shard_map/reduce_sum | solution.py:37
  230.7 0.3 fusion.22
  231.0 0.5 multiply_reduce_fusion.1
  231.8 2.9 fusion.6
  234.7 3.9 %collective-permute-start = (bf16[128,2048]{1,0:T(8,128)(2,1)S(1)}, bf16[128,2048]{1,0:T(8,128)(2,1)S(1)}, u32[]{:S(2)}, u32[]{:S(2)}) collective-permute-start(bf16[128,2048]{1,0:T(8,128)(2,1)S(1)} %fusion.6), channel_id=1, source_target_pairs={{0,16},{16,32},{32,48},{48,64},{64,80},{80,96},{96,112},{112,128},... | collective-permute-start | bytes 1572872 | tf_op jit(solution)/shard_map/ppermute | solution.py:10
  238.6 5.9 %collective-permute-done = bf16[128,2048]{1,0:T(8,128)(2,1)S(1)} collective-permute-done((bf16[128,2048]{1,0:T(8,128)(2,1)S(1)}, bf16[128,2048]{1,0:T(8,128)(2,1)S(1)}, u32[]{:S(2)}, u32[]{:S(2)}) %collective-permute-start) | collective-permute-done | bytes 524320 | tf_op jit(solution)/shard_map/ppermute | solution.py:10
  244.8 6.5 %fusion = f32[128,3072]{1,0:T(8,128)S(1)} fusion(bf16[1,2048,3072]{2,1,0:T(8,128)(2,1)} %all-gather.7.cloned.1.call-done, bf16[128,2048]{1,0:T(8,128)(2,1)S(1)} %get-tuple-element.7, f32[128]{0:T(128)S(1)} %add_rsqrt_fusion.2, f32[2048]{0:T(1024)S(1)} %bitcast.91), kind=kOutput, calls=%fused_computation | convolution fusion | flops 1611661312 | bytes 14688768 | tf_op jit(solution)/shard_map/dot_general | solution.py:22
  251.4 0.3 fusion.39
  252.0 1.0 convolution_convert_fusion
  253.1 68.6 %all-gather.11.cloned.1.call-done = bf16[128,128,128]{2,1,0:T(8,128)(2,1)} async-done(((bf16[8,128,128]{2,1,0:T(8,128)(2,1)}), bf16[128,128,128]{2,1,0:T(8,128)(2,1)}) %all-gather.11.cloned.1.call-update) | async-done | bytes 4194320 | tf_op jit(solution)/shard_map/all_gather | solution.py:31
  321.7 3.5 %convert_reduce_fusion = (f32[8,128,128]{2,1,0:T(8,128)S(1)}, f32[8,128,128]{2,1,0:T(8,128)S(1)}) fusion(bf16[16,8,128,128]{3,2,1,0:T(8,128)(2,1)} %bitcast.79, f32[16]{0:T(128)S(1)} %compare_convert_fusion), kind=kLoop, calls=%fused_computation.4 | loop fusion | flops 8126464 | bytes 5242944 | tf_op jit(solution)/shard_map/reduce_sum | solution.py:37
  325.2 0.9 bitcast_add_fusion
  326.1 0.3 fusion.24
  326.5 0.5 multiply_reduce_fusion
  327.1 3.7 %fusion.8 = bf16[1,128,2048]{2,1,0:T(8,128)(2,1)} fusion(bf16[128,1024]{0,1:T(8,128)(2,1)S(1)} %bitcast.89, bf16[1024,2048]{1,0:T(8,128)(2,1)} %bitcast.11, bf16[128,2048]{1,0:T(8,128)(2,1)S(1)} %get-tuple-element.7), kind=kOutput, calls=%fused_computation.14 | convolution fusion | flops 537657344 | bytes 5505024 | tf_op jit(solution)/shard_map/dot_general | solution.py:49
  (33 shorter events, 1.7 us)
Async XLA Ops:
  7.2 114.5 %all-gather.7.cloned.1.call-start = ((), (), s32[]{:S(2)}) async-start(), calls=%async_computation.1 | async-start | bytes 13369344 | tf_op jit(solution)/shard_map/all_gather | solution.py:65
  7.9 219.2 %all-gather.9.cloned.1.call-start = ((), (), s32[]{:S(2)}) async-start(), calls=%async_computation.2 | async-start | bytes 4456448 | tf_op jit(solution)/shard_map/all_gather | solution.py:31
  128.4 1.7 copy-start.4
  132.6 99.2 %all-to-all-start = ((bf16[16,64,2048]{2,1,0:T(8,128)(2,1)}), bf16[16,64,2048]{2,1,0:T(8,128)(2,1)}, u32[]{:S(2)}, u32[]{:S(2)}) async-start(bf16[16,64,2048]{2,1,0:T(8,128)(2,1)} %stack.3), calls=%async_computation | async-start | bytes 8388608 | tf_op jit(solution)/shard_map/all_to_all | solution.py:59
  137.6 93.1 %copy-start.1 = (f32[1,8,128,128]{3,2,1,0:T(8,128)S(1)}, f32[1,8,128,128]{3,2,1,0:T(8,128)}, u32[]{:S(2)}) copy-start(f32[1,8,128,128]{3,2,1,0:T(8,128)} %param.9) | copy-start | bytes 1572868
  137.6 184.1 %all-gather.11.cloned.1.call-start = ((), (), s32[]{:S(2)}) async-start(), calls=%async_computation.3 | async-start | bytes 4456448 | tf_op jit(solution)/shard_map/all_gather | solution.py:31
  227.1 4.4 %copy-start.5 = (f32[1,1024]{1,0:T(1,128)S(1)}, f32[1,1024]{1,0:T(1,128)}, u32[]{:S(2)}) copy-start(f32[1,1024]{1,0:T(1,128)} %param.13) | copy-start | bytes 12292
  227.1 4.7 %copy-start = (bf16[1,128,2048]{2,1,0:T(8,128)(2,1)S(1)}, bf16[1,128,2048]{2,1,0:T(8,128)(2,1)}, u32[]{:S(2)}) copy-start(bf16[1,128,2048]{2,1,0:T(8,128)(2,1)} %param.7) | copy-start | bytes 1572868
  231.5 13.1 %copy-start.2 = (bf16[128,2048]{1,0:T(8,128)(2,1)S(1)}, bf16[128,2048]{1,0:T(8,128)(2,1)}, u32[]{:S(2)}) copy-start(bf16[128,2048]{1,0:T(8,128)(2,1)} %param.8) | copy-start | bytes 1572868
  231.5 13.4 %copy-start.3 = (f32[1,2048]{1,0:T(1,128)S(1)}, f32[1,2048]{1,0:T(1,128)}, u32[]{:S(2)}) copy-start(f32[1,2048]{1,0:T(1,128)} %param.12) | copy-start | bytes 24580
  234.7 9.9 %collective-permute-start = (bf16[128,2048]{1,0:T(8,128)(2,1)S(1)}, bf16[128,2048]{1,0:T(8,128)(2,1)S(1)}, u32[]{:S(2)}, u32[]{:S(2)}) collective-permute-start(bf16[128,2048]{1,0:T(8,128)(2,1)S(1)} %fusion.6), channel_id=1, source_target_pairs={{0,16},{16,32},{32,48},{48,64},{64,80},{80,96},{96,112},{112,128},... | collective-permute-start | bytes 1572872 | tf_op jit(solution)/shard_map/ppermute | solution.py:10
Sparse Core Ops, SparseCore 0:
  11.0 110.6 all-gather.6
  130.2 96.8 all-gather.8
  253.2 68.4 all-gather.10
